TPU v7x, 512 devices: a whole 4x8x8 slice. The times are simulated.
512 devices in a mesh: shot: 8 (over z_lo, core), space: 64 (over y, z_hi, x).
Axes of the slice: x: 4, y: 8, z: 8 (z_hi: 2, z_lo: 4; z = z_hi * 4 + z_lo), core: 2. Of those that a mesh axis runs over, the one named last changes fastest.
Arguments:
- velocity_term: float32 [512, 64, 128], P('space'), may hold values from 0.05 to 0.2
- forward_previous: float32 [8, 512, 64, 128], P('shot', 'space'), may hold values from -6 to 6
- forward_current: float32 [8, 512, 64, 128], P('shot', 'space'), may hold values from -6 to 6
- adjoint_previous: float32 [8, 512, 64, 128], P('shot', 'space'), may hold values from -6 to 6
- adjoint_current: float32 [8, 512, 64, 128], P('shot', 'space'), may hold values from -6 to 6
- source_cell: int32 [8], P('shot'), may hold values from 0 to 4194303
- wavelet: float32 [8, 2], P('shot'), may hold values from -40 to 40
- trace_cells: int32 [8, 512, 8], P('shot'), may hold values from 0 to 4194303, as said below
- trace_weights: float32 [8, 512, 8], P('shot'), may hold values from -2 to 2
- observed: float32 [8, 2, 512], P('shot', None, 'space'), may hold values from -6 to 6
Outputs:
- forward_next: float32 [8, 512, 64, 128], P('shot', 'space')
- adjoint_next: float32 [8, 512, 64, 128], P('shot', 'space')
- residual: float32 [8, 2, 512], P('shot', None, 'space')
- gradient: float32 [512, 64, 128], P('space', 'shot')
Inputs may be any that keep to these rules, and one draw needn't show every extreme that they name: `trace_cells`: each trace's footprint is 8 cells in a row along the first dimension at one position of the other two; a trace lies in the first quarter of the first dimension with chance about one half.
All inputs are finite; a program needn't handle non-finite values.
Results may differ from a plain program's by a relative error of at most 0.0001.
Values sent between devices are 32-bit elements; how exact they have to be, the bound alone decides.
A program may use at most 64 MiB of HBM per device.

v0:
```python
import jax
import jax.numpy as jnp
from jax import lax
from jax.sharding import PartitionSpec as P

coeffs = (-205.0 / 72.0, 8.0 / 5.0, -1.0 / 5.0, 8.0 / 315.0, -1.0 / 560.0)


def padded_2(cells, sides, width):
    for axis, dim in sides:
        count = lax.axis_size(axis)
        ends = count - 1
        head = lax.slice_in_dim(cells, 0, width, axis=dim)
        tail = lax.slice_in_dim(cells, cells.shape[dim] - width, cells.shape[dim], axis=dim)
        cells = jnp.concatenate(
            [
                lax.ppermute(tail, axis, [(i, (i + 1) % count) for i in range(ends)]),
                cells,
                lax.ppermute(head, axis, [((i + 1) % count, i) for i in range(ends)]),
            ],
            axis=dim,
        )
    return cells


def laplace_ext(field):
    count = field.shape[0] - 8
    core = field[4 : 4 + count]
    width_y = core.shape[1]
    width_z = core.shape[2]
    padded = jnp.pad(core, ((0, 0), (4, 4), (4, 4)))
    result = 3.0 * coeffs[0] * core
    for j in range(1, 5):
        along_x = field[4 + j : 4 + j + count] + field[4 - j : 4 - j + count]
        along_y = (
            padded[:, 4 + j : 4 + j + width_y, 4 : 4 + width_z]
            + padded[:, 4 - j : 4 - j + width_y, 4 : 4 + width_z]
        )
        along_z = (
            padded[:, 4 : 4 + width_y, 4 + j : 4 + j + width_z]
            + padded[:, 4 : 4 + width_y, 4 - j : 4 - j + width_z]
        )
        result = result + coeffs[j] * (along_x + along_y + along_z)
    return result


def per_device(
    velocity_term,
    forward_previous,
    forward_current,
    adjoint_previous,
    adjoint_current,
    source_cell,
    wavelet,
    trace_cells,
    trace_weights,
    observed,
):
    slab_x, width_y, width_z = velocity_term.shape
    plane = width_y * width_z
    anchor = lax.axis_index("space") * slab_x
    weights = trace_weights[0]

    def add_at(field, speed, start_x, cells, amounts):
        count = field.shape[0] * plane
        local = cells - start_x * plane
        inside = (local >= 0) & (local < count)
        clipped = jnp.clip(local, 0, count - 1)
        adds = jnp.where(inside, speed.reshape(-1)[clipped] * amounts, 0.0)
        flat = field.reshape(-1).at[clipped.reshape(-1)].add(adds.reshape(-1))
        return flat.reshape(field.shape)

    def add_source(field, speed, start_x, amount):
        return add_at(field, speed, start_x, source_cell[0].reshape(1), amount.reshape(1))

    def add_inject(field, speed, start_x, values):
        return add_at(field, speed, start_x, trace_cells[0], weights * values[:, None])

    own_local = trace_cells[0] - anchor * plane
    own_inside = (own_local >= 0) & (own_local < slab_x * plane)
    own_clipped = jnp.clip(own_local, 0, slab_x * plane - 1)

    def sample(field):
        return jnp.sum(
            jnp.where(own_inside, field.reshape(-1)[own_clipped] * weights, 0.0), axis=-1
        )

    p_before = forward_previous[0]
    p_now = forward_current[0]
    a_before = adjoint_previous[0]
    a_now = adjoint_current[0]
    first = padded_2(jnp.stack([p_now, a_now]), (("space", 1),), 4)
    lap_zero = laplace_ext(first[0])
    lap_adjoint = laplace_ext(first[1])
    p_one = add_source(
        2.0 * p_now - p_before + velocity_term * lap_zero, velocity_term, anchor, wavelet[0, 0]
    )
    lap_one = laplace_ext(padded_2(p_one, (("space", 0),), 4))
    p_two = add_source(
        2.0 * p_one - p_now + velocity_term * lap_one, velocity_term, anchor, wavelet[0, 1]
    )
    partials = jnp.stack([sample(p_one), sample(p_two)])
    synthetic_own = lax.psum_scatter(partials, "space", scatter_dimension=1, tiled=True)
    misfit_own = synthetic_own - observed[0]
    misfit_all = lax.all_gather(misfit_own, "space", axis=1, tiled=True)
    a_one = add_inject(
        2.0 * a_now - a_before + velocity_term * lap_adjoint, velocity_term, anchor, misfit_all[1]
    )
    lap_adj_one = laplace_ext(padded_2(a_one, (("space", 0),), 4))
    a_two = add_inject(
        2.0 * a_one - a_now + velocity_term * lap_adj_one, velocity_term, anchor, misfit_all[0]
    )
    terms = a_one * lap_one + a_two * lap_zero
    scale = 1.0 / (lax.axis_size("shot") * forward_current.shape[0])
    gradient = lax.psum_scatter(terms, "shot", scatter_dimension=1, tiled=True) * scale
    return (p_two[None], a_two[None], misfit_own[None], gradient)


def solution(mesh):
    placed = (
        P("space", None, None),
        P("shot", "space", None, None),
        P("shot", "space", None, None),
        P("shot", "space", None, None),
        P("shot", "space", None, None),
        P("shot"),
        P("shot", None),
        P("shot", None, None),
        P("shot", None, None),
        P("shot", None, "space"),
    )
    return jax.shard_map(
        per_device,
        mesh=mesh,
        in_specs=placed,
        out_specs=(
            P("shot", "space", None, None),
            P("shot", "space", None, None),
            P("shot", None, "space"),
            P("space", "shot", None),
        ),
        check_vma=False,
    )
```

profile of v0, /device:TPU:10, one launch (start us, length us, event | category | flops | bytes accessed | tf_op | source)
XLA Modules:
  0.0 707.6 jit_solution(15188208120196253433)
XLA Ops:
  7.2 1.0 constant_dynamic-update-slice_fusion.1
  8.3 3.4 collective-permute-start.1
  11.7 2.4 collective-permute-start
  15.9 0.6 compare_select_fusion.1
  17.3 0.7 squeeze.29
  18.6 40.5 %gather_fusion = f32[4096]{0:T(1024)} fusion(f32[65536]{0:T(1024)S(1)} %bitcast.176, s32[4096]{0:T(1024)S(1)} %broadcast_clamp_fusion), kind=kCustom, calls=%fused_computation | custom fusion | bytes 49152 | tf_op jit(solution)/shard_map/gather | solution.py:69
  59.1 1.3 dynamic-slice.21
  61.0 0.6 fusion.167
  61.7 1.3 fusion.154
  63.0 2.1 fusion.155
  65.1 23.0 %gather_fusion.1 = f32[4096]{0:T(1024)S(1)} fusion(f32[65536]{0:T(1024)S(1)} %fusion.155, s32[4096]{0:T(1024)S(1)} %broadcast_clamp_fusion), kind=kCustom, calls=%fused_computation.1 | custom fusion | bytes 49152 | tf_op jit(solution)/shard_map/gather | solution.py:85
  88.2 3.5 collective-permute-start.3
  91.7 10.0 %collective-permute-start.2 = (f32[4,64,128]{2,1,0:T(8,128)S(1)}, f32[4,64,128]{2,1,0:T(8,128)S(1)}, u32[]{:S(2)}, u32[]{:S(2)}) collective-permute-start(f32[4,64,128]{2,1,0:T(8,128)S(1)} %bitcast.193), channel_id=1, source_target_pairs={{1,0},{2,1},{3,2},{4,3},{5,4},{6,5},{7,6},{8,7},{9,8},{10,9},{11,1... | collective-permute-start | bytes 393224 | tf_op jit(solution)/shard_map/ppermute | solution.py:19
  102.0 0.6 fusion.55
  103.0 1.6 collective-permute-done.2
  104.7 0.6 multiply_add_fusion.1
  105.3 2.2 fusion.156
  107.5 23.0 %gather_fusion.2 = f32[4096]{0:T(1024)S(1)} fusion(f32[65536]{0:T(1024)S(1)} %fusion.156, s32[4096]{0:T(1024)S(1)} %broadcast_clamp_fusion), kind=kCustom, calls=%fused_computation.2 | custom fusion | bytes 49152 | tf_op jit(solution)/shard_map/gather | solution.py:85
  130.7 0.8 copy-done.6
  131.9 206.5 %all-reduce.4 = f32[2,512]{1,0:T(2,128)S(1)} all-reduce(f32[2,512]{1,0:T(2,128)S(1)} %pad_maximum_fusion.6), channel_id=2, replica_groups=mesh['shot'=8,'space'=64] {'space'}, use_global_device_ids=true, to_apply=%region_2.3.clone | all-reduce | flops 1024 | bytes 8192
  338.4 0.6 fusion.159
  339.1 203.5 %all-gather = f32[64,8,2]{1,2,0:T(2,128)S(1)} all-gather(f32[1,8,2]{1,2,0:T(2,128)S(1)} %get-tuple-element.57), channel_id=1, replica_groups=mesh['shot'=8,'space'=64] {'space'}, dimensions={0}, use_global_device_ids=true | all-gather | bytes 4160 | tf_op jit(solution)/shard_map/all_gather | solution.py:105
  543.9 28.0 %scatter_fusion = f32[65536]{0:T(1024)S(1)} fusion(f32[65536]{0:T(1024)S(1)} %bitcast.183, s32[4096]{0:T(1024)S(1)} %bitcast.191, f32[4096]{0:T(1024)S(1)} %get-tuple-element.55), kind=kCustom, calls=%fused_computation.3 | custom fusion | flops 4096 | bytes 65536 | tf_op jit(solution)/shard_map/scatter-add | solution.py:70
  571.9 1.9 collective-permute-start.5
  573.8 3.9 collective-permute-start.4
  577.7 1.0 collective-permute-done.5
  578.7 1.9 collective-permute-done.4
  580.7 0.6 fusion.8
  581.3 28.0 %scatter_fusion.1 = f32[65536]{0:T(1024)S(1)} fusion(f32[65536]{0:T(1024)S(1)} %bitcast.186, s32[4096]{0:T(1024)S(1)} %bitcast.192, f32[4096]{0:T(1024)S(1)} %get-tuple-element.54), kind=kCustom, calls=%fused_computation.4 | custom fusion | flops 4096 | bytes 65536 | tf_op jit(solution)/shard_map/scatter-add | solution.py:70
  609.3 0.8 multiply_add_fusion
  610.1 89.3 %reduce-scatter.3.cloned.1.call-done = f32[8,8,128]{2,1,0:T(8,128)} async-done(((f32[8,64,128]{2,1,0:T(8,128)}), f32[8,8,128]{2,1,0:T(8,128)}) %reduce-scatter.3.cloned.1.call-update) | async-done | bytes 32784 | tf_op jit(solution)/shard_map/reduce_scatter | solution.py:115
  699.4 1.4 broadcast_multiply_fusion
  (67 shorter events, 4.5 us)
Async XLA Ops:
  7.2 1.1 copy-start.7
  7.2 692.2 %reduce-scatter.3.cloned.1.call-start = ((), (), s32[]{:S(2)}) async-start(), calls=%async_computation.1 | async-start | bytes 294912 | tf_op jit(solution)/shard_map/reduce_scatter | solution.py:115
  8.3 6.5 copy-start.16
  8.3 53.3 %collective-permute-start.1 = (f32[2,4,64,128]{3,2,1,0:T(8,128)S(1)}, f32[2,4,64,128]{3,2,1,0:T(8,128)S(1)}, u32[]{:S(2)}, u32[]{:S(2)}) collective-permute-start(f32[2,4,64,128]{3,2,1,0:T(8,128)S(1)} %get-tuple-element.49), channel_id=1, source_target_pairs={{0,1},{1,2},{2,3},{3,4},{4,5},{5,6},{6,7},{7,8},{8,9},{9,10},{10,1... | collective-permute-start | bytes 786440 | tf_op jit(solution)/shard_map/ppermute | solution.py:17
  11.7 49.9 %collective-permute-start = (f32[2,4,64,128]{3,2,1,0:T(8,128)S(1)}, f32[2,4,64,128]{3,2,1,0:T(8,128)S(1)}, u32[]{:S(2)}, u32[]{:S(2)}) collective-permute-start(f32[2,4,64,128]{3,2,1,0:T(8,128)S(1)} %get-tuple-element.48), channel_id=1, source_target_pairs={{1,0},{2,1},{3,2},{4,3},{5,4},{6,5},{7,6},{8,7},{9,8},{10,9},{11,1... | collective-permute-start | bytes 786440 | tf_op jit(solution)/shard_map/ppermute | solution.py:19
  15.0 0.7 copy-start.9
  16.5 0.7 copy-start.17
  17.2 1.4 copy-start
  17.3 41.8 %copy-start.5 = (f32[1,512,8]{2,1,0:T(8,128)}, f32[1,512,8]{2,1,0:T(8,128)S(1)}, u32[]{:S(2)}) copy-start(f32[1,512,8]{2,1,0:T(8,128)S(1)} %copy.19) | copy-start | bytes 49156
  18.6 43.1 %copy-start.4 = (f32[1,8,64,128]{3,2,1,0:T(8,128)S(1)}, f32[1,8,64,128]{3,2,1,0:T(8,128)}, u32[]{:S(2)}) copy-start(f32[1,8,64,128]{3,2,1,0:T(8,128)} %param.16) | copy-start | bytes 786436
  18.6 43.1 %copy-start.12 = (f32[1,8,64,128]{3,2,1,0:T(8,128)S(1)}, f32[1,8,64,128]{3,2,1,0:T(8,128)}, u32[]{:S(2)}) copy-start(f32[1,8,64,128]{3,2,1,0:T(8,128)} %param.15) | copy-start | bytes 786436
  60.4 0.7 copy-start.18
  65.1 36.8 %copy-start.13 = (f32[1,8,64,128]{3,2,1,0:T(8,128)S(1)}, f32[1,8,64,128]{3,2,1,0:T(8,128)}, u32[]{:S(2)}) copy-start(f32[1,8,64,128]{3,2,1,0:T(8,128)} %param.17) | copy-start | bytes 786436
  88.2 13.8 %copy-start.8 = (f32[1,8,64,128]{3,2,1,0:T(8,128)S(1)}, f32[1,8,64,128]{3,2,1,0:T(8,128)}, u32[]{:S(2)}) copy-start(f32[1,8,64,128]{3,2,1,0:T(8,128)} %param.18) | copy-start | bytes 786436
  88.2 14.8 %collective-permute-start.3 = (f32[4,64,128]{2,1,0:T(8,128)S(1)}, f32[4,64,128]{2,1,0:T(8,128)S(1)}, u32[]{:S(2)}, u32[]{:S(2)}) collective-permute-start(f32[4,64,128]{2,1,0:T(8,128)S(1)} %bitcast.194), channel_id=1, source_target_pairs={{0,1},{1,2},{2,3},{3,4},{4,5},{5,6},{6,7},{7,8},{8,9},{9,10},{10,1... | collective-permute-start | bytes 393224 | tf_op jit(solution)/shard_map/ppermute | solution.py:17
  91.7 13.0 %collective-permute-start.2 = (f32[4,64,128]{2,1,0:T(8,128)S(1)}, f32[4,64,128]{2,1,0:T(8,128)S(1)}, u32[]{:S(2)}, u32[]{:S(2)}) collective-permute-start(f32[4,64,128]{2,1,0:T(8,128)S(1)} %bitcast.193), channel_id=1, source_target_pairs={{1,0},{2,1},{3,2},{4,3},{5,4},{6,5},{7,6},{8,7},{9,8},{10,9},{11,1... | collective-permute-start | bytes 393224 | tf_op jit(solution)/shard_map/ppermute | solution.py:19
  107.5 23.0 %copy-start.1 = (f32[65536]{0:T(1024)}, f32[65536]{0:T(1024)S(1)}, u32[]{:S(2)}) copy-start(f32[65536]{0:T(1024)S(1)} %fusion.156) | copy-start | bytes 786436
  107.5 23.2 %copy-start.10 = (s32[1,512,8]{2,1,0:T(8,128)S(1)}, s32[1,512,8]{2,1,0:T(8,128)}, u32[]{:S(2)}) copy-start(s32[1,512,8]{2,1,0:T(8,128)} %copy-done.9) | copy-start | bytes 49156
  130.5 1.0 copy-start.6
  130.5 413.3 %copy-start.14 = (s32[4096,1]{0,1:T(1,128)S(1)}, s32[4096,1]{0,1:T(1,128)}, u32[]{:S(2)}) copy-start(s32[4096,1]{0,1:T(1,128)} %compare_select_fusion.1) | copy-start | bytes 49156
  131.9 206.5 %copy-start.19 = (f32[1,2,8]{2,1,0:T(2,128)S(1)}, f32[1,2,8]{2,1,0:T(2,128)}, u32[]{:S(2)}) copy-start(f32[1,2,8]{2,1,0:T(2,128)} %param.23) | copy-start | bytes 196
  543.1 0.7 copy-start.3
  543.1 0.7 copy-start.15
  571.9 6.9 collective-permute-start.5
  573.8 6.9 collective-permute-start.4
  581.3 28.0 %copy-start.11 = (f32[8,64,128]{2,1,0:T(8,128)S(1)}, f32[8,64,128]{2,1,0:T(8,128)}, u32[]{:S(2)}) copy-start(f32[8,64,128]{2,1,0:T(8,128)} %get-tuple-element.47) | copy-start | bytes 786436
  609.3 0.8 copy-start.2
Sparse Core Ops, SparseCore 0:
  610.2 89.1 reduce-scatter.2
where the time goes:
time: 708 us
  blocking collectives  410 us (58%)
  local copies, waits for them, and re-layouts  94.6 us (13%)
  waiting for transfers between devices  94.4 us (13%)
  other arithmetic  67.1 us (9%)
  starting transfers between devices  25.3 us (4%)
  between operations  16.2 us (2%)
    unnamed x1, blocking collectives  207 us
    all_gather x1, blocking collectives, per_device(): misfit_all = lax.all_gather(misfit_own, 'space', axis=1, tiled=True)  204 us
    reduce_scatter x1, waiting for transfers between devices, per_device(): lax.psum_scatter(terms, 'shot', scatter_dimension=1, tiled=True) * scale  89.3 us
    scatter-add x4, other arithmetic, add_at(): flat = field.reshape(-1).at[clipped.reshape(-1)].add(adds.reshape(-1))  60.2 us
    gather x4, local copies, waits for them, and re-layouts, sample(): field.reshape(-1)[own_clipped] * weights  46.4 us
    gather x1, local copies, waits for them, and re-layouts, add_at(): adds = jnp.where(inside, speed.reshape(-1)[clipped] * amounts, 0.0)  40.5 us
    ppermute x3, starting transfers between devices, padded_2(): lax.ppermute(head, axis, [((i + 1) % count, i) for i in range(ends)])  16.4 us
  transfers between devices with their start and end apart: 7, of which 5 were waited for; matrix products, arithmetic and copies ran while one was open for 6% of the time, Pallas kernels for 0%

commit v1 on v0

--- a/solution.py
+++ b/solution.py
@@ -102,7 +102,10 @@
     partials = jnp.stack([sample(p_one), sample(p_two)])
     synthetic_own = lax.psum_scatter(partials, "space", scatter_dimension=1, tiled=True)
     misfit_own = synthetic_own - observed[0]
-    misfit_all = lax.all_gather(misfit_own, "space", axis=1, tiled=True)
+    size = lax.axis_size("space")
+    blocks = jnp.stack([misfit_own for _ in range(size)])
+    blocks = lax.all_to_all(blocks, "space", split_axis=0, concat_axis=0)
+    misfit_all = jnp.concatenate(blocks, axis=1)
     a_one = add_inject(
         2.0 * a_now - a_before + velocity_term * lap_adjoint, velocity_term, anchor, misfit_all[1]
     )

time: 708 us -> 511 us (0.72)
  the two profiles are of different devices: /device:TPU:10 before, /device:TPU:2 now
where the time goes in v1:
time: 511 us; the launch traced here: 510 us
  blocking collectives  218 us (43%)
  local copies, waits for them, and re-layouts  96.3 us (19%)
  other arithmetic  68.6 us (13%)
  waiting for transfers between devices  61.5 us (12%)
  starting transfers between devices  48.8 us (10%)
  between operations  16.4 us (3%)
    unnamed x1, blocking collectives  218 us
    scatter-add x4, other arithmetic, add_at(): flat = field.reshape(-1).at[clipped.reshape(-1)].add(adds.reshape(-1))  61.1 us
    gather x4, local copies, waits for them, and re-layouts, sample(): field.reshape(-1)[own_clipped] * weights  46.4 us
    reduce_scatter x1, waiting for transfers between devices, per_device(): lax.psum_scatter(terms, 'shot', scatter_dimension=1, tiled=True) * scale  45.4 us
    gather x1, local copies, waits for them, and re-layouts, add_at(): adds = jnp.where(inside, speed.reshape(-1)[clipped] * amounts, 0.0)  40.3 us
    all_to_all x1, starting transfers between devices, per_device(): blocks = lax.all_to_all(blocks, 'space', split_axis=0, concat_axis=0)  21.5 us
    ppermute x3, starting transfers between devices, padded_2(): lax.ppermute(tail, axis, [(i, (i + 1) % count) for i in range(ends)])  16 us
    all_to_all x1, waiting for transfers between devices, per_device(): blocks = lax.all_to_all(blocks, 'space', split_axis=0, concat_axis=0)  12.6 us
  transfers between devices with their start and end apart: 8, of which 5 were waited for; matrix products, arithmetic and copies ran while one was open for 13% of the time, Pallas kernels for 0%

profile of v1, /device:TPU:2, one launch (start us, length us, event | category | flops | bytes accessed | tf_op | source)
XLA Modules:
  0.0 509.9 jit_solution(3703127428159719327)
XLA Ops:
  7.2 1.0 constant_dynamic-update-slice_fusion.1
  8.3 3.4 collective-permute-start.1
  11.7 5.7 %collective-permute-start = (f32[2,4,64,128]{3,2,1,0:T(8,128)S(1)}, f32[2,4,64,128]{3,2,1,0:T(8,128)S(1)}, u32[]{:S(2)}, u32[]{:S(2)}) collective-permute-start(f32[2,4,64,128]{3,2,1,0:T(8,128)S(1)} %get-tuple-element.50), channel_id=1, source_target_pairs={{1,0},{2,1},{3,2},{4,3},{5,4},{6,5},{7,6},{8,7},{9,8},{10,9},{11,1... | collective-permute-start | bytes 786440 | tf_op jit(solution)/shard_map/ppermute | solution.py:19
  18.5 0.6 compare_select_fusion.1
  21.4 1.3 fusion.154
  22.7 2.2 fusion.155
  24.9 0.7 fusion.163
  25.6 10.3 %collective-permute-start.3 = (f32[4,64,128]{2,1,0:T(8,128)}, f32[4,64,128]{2,1,0:T(8,128)}, u32[]{:S(2)}, u32[]{:S(2)}) collective-permute-start(f32[4,64,128]{2,1,0:T(8,128)} %bitcast.15), channel_id=1, source_target_pairs={{0,1},{1,2},{2,3},{3,4},{4,5},{5,6},{6,7},{7,8},{8,9},{9,10},{10,1... | collective-permute-start | bytes 393224 | tf_op jit(solution)/shard_map/ppermute | solution.py:17
  35.9 1.9 collective-permute-start.2
  37.8 40.3 %gather_fusion = f32[4096]{0:T(1024)} fusion(f32[65536]{0:T(1024)S(1)} %bitcast.164, s32[4096]{0:T(1024)S(1)} %broadcast_clamp_fusion), kind=kCustom, calls=%fused_computation | custom fusion | bytes 49152 | tf_op jit(solution)/shard_map/gather | solution.py:69
  78.2 0.8 squeeze.29
  78.9 1.3 dynamic-slice.21
  80.9 23.0 %gather_fusion.1 = f32[4096]{0:T(1024)S(1)} fusion(f32[65536]{0:T(1024)S(1)} %fusion.155, s32[4096]{0:T(1024)S(1)} %broadcast_clamp_fusion), kind=kCustom, calls=%fused_computation.1 | custom fusion | bytes 49152 | tf_op jit(solution)/shard_map/gather | solution.py:85
  104.1 0.8 copy-done.7
  104.9 1.8 multiply_add_fusion.1
  106.7 2.1 fusion.156
  108.8 23.0 %gather_fusion.2 = f32[4096]{0:T(1024)S(1)} fusion(f32[65536]{0:T(1024)S(1)} %fusion.156, s32[4096]{0:T(1024)S(1)} %broadcast_clamp_fusion), kind=kCustom, calls=%fused_computation.2 | custom fusion | bytes 49152 | tf_op jit(solution)/shard_map/gather | solution.py:85
  132.0 0.8 copy-done.9
  133.1 218.4 %all-reduce.4 = f32[2,512]{1,0:T(2,128)S(1)} all-reduce(f32[2,512]{1,0:T(2,128)S(1)} %pad_maximum_fusion.6), channel_id=2, replica_groups=mesh['shot'=8,'space'=64] {'space'}, use_global_device_ids=true, to_apply=%region_2.3.clone | all-reduce | flops 1024 | bytes 8192
  351.6 0.6 stack.16
  352.2 21.5 %all-to-all-start = ((f32[64,2,8]{2,1,0:T(2,128)}), f32[64,2,8]{2,1,0:T(2,128)S(1)}, u32[]{:S(2)}, u32[]{:S(2)}) async-start(f32[64,2,8]{2,1,0:T(2,128)} %stack.16), calls=%async_computation | async-start | bytes 131072 | tf_op jit(solution)/shard_map/all_to_all | solution.py:107
  373.9 0.6 fusion.55
  374.7 12.6 %all-to-all-done = f32[64,2,8]{2,1,0:T(2,128)S(1)} async-done(((f32[64,2,8]{2,1,0:T(2,128)}), f32[64,2,8]{2,1,0:T(2,128)S(1)}, u32[]{:S(2)}, u32[]{:S(2)}) %all-to-all-start) | async-done | bytes 4128 | tf_op jit(solution)/shard_map/all_to_all | solution.py:107
  388.8 28.4 %scatter_fusion = f32[65536]{0:T(1024)S(1)} fusion(f32[65536]{0:T(1024)S(1)} %bitcast.170, s32[4096]{0:T(1024)S(1)} %bitcast.179, f32[4096]{0:T(1024)S(1)} %get-tuple-element.57), kind=kCustom, calls=%fused_computation.3 | custom fusion | flops 4096 | bytes 65536 | tf_op jit(solution)/shard_map/scatter-add | solution.py:70
  417.2 2.4 collective-permute-start.5
  419.6 3.5 collective-permute-start.4
  423.1 1.0 collective-permute-done.5
  424.1 2.4 collective-permute-done.4
  427.1 28.4 %scatter_fusion.1 = f32[65536]{0:T(1024)S(1)} fusion(f32[65536]{0:T(1024)S(1)} %bitcast.173, s32[4096]{0:T(1024)S(1)} %bitcast.180, f32[4096]{0:T(1024)S(1)} %get-tuple-element.56), kind=kCustom, calls=%fused_computation.4 | custom fusion | flops 4096 | bytes 65536 | tf_op jit(solution)/shard_map/scatter-add | solution.py:70
  455.5 0.8 multiply_add_fusion
  456.3 45.4 %reduce-scatter.3.cloned.1.call-done = f32[8,8,128]{2,1,0:T(8,128)} async-done(((f32[8,64,128]{2,1,0:T(8,128)}), f32[8,8,128]{2,1,0:T(8,128)}) %reduce-scatter.3.cloned.1.call-update) | async-done | bytes 32784 | tf_op jit(solution)/shard_map/reduce_scatter | solution.py:118
  501.7 1.4 broadcast_multiply_fusion
  (85 shorter events, 5.1 us)
Async XLA Ops:
  7.2 1.0 copy-start.10
  8.2 13.1 %copy-start.3 = (f32[2,8,64,128]{3,2,1,0:T(8,128)}, f32[2,8,64,128]{3,2,1,0:T(8,128)S(1)}, u32[]{:S(2)}) copy-start(f32[2,8,64,128]{3,2,1,0:T(8,128)S(1)} %constant_dynamic-update-slice_fusion) | copy-start | bytes 1572868
  8.2 9.2 %copy-start.23 = (s32[1,512,8]{1,2,0:T(8,128)S(1)}, s32[1,512,8]{1,2,0:T(8,128)}, u32[]{:S(2)}) copy-start(s32[1,512,8]{1,2,0:T(8,128)} %param.21) | copy-start | bytes 49156
  8.3 13.0 %collective-permute-start.1 = (f32[2,4,64,128]{3,2,1,0:T(8,128)S(1)}, f32[2,4,64,128]{3,2,1,0:T(8,128)S(1)}, u32[]{:S(2)}, u32[]{:S(2)}) collective-permute-start(f32[2,4,64,128]{3,2,1,0:T(8,128)S(1)} %get-tuple-element.51), channel_id=1, source_target_pairs={{0,1},{1,2},{2,3},{3,4},{4,5},{5,6},{6,7},{7,8},{8,9},{9,10},{10,1... | collective-permute-start | bytes 786440 | tf_op jit(solution)/shard_map/ppermute | solution.py:17
  11.7 9.7 %collective-permute-start = (f32[2,4,64,128]{3,2,1,0:T(8,128)S(1)}, f32[2,4,64,128]{3,2,1,0:T(8,128)S(1)}, u32[]{:S(2)}, u32[]{:S(2)}) collective-permute-start(f32[2,4,64,128]{3,2,1,0:T(8,128)S(1)} %get-tuple-element.50), channel_id=1, source_target_pairs={{1,0},{2,1},{3,2},{4,3},{5,4},{6,5},{7,6},{8,7},{9,8},{10,9},{11,1... | collective-permute-start | bytes 786440 | tf_op jit(solution)/shard_map/ppermute | solution.py:19
  18.3 3.1 copy-start.19
  18.5 1.5 copy-start.24
  19.7 1.6 copy-start
  19.8 1.6 copy-start.6
  20.1 58.1 %copy-start.8 = (f32[1,512,8]{2,1,0:T(8,128)}, f32[1,512,8]{2,1,0:T(8,128)S(1)}, u32[]{:S(2)}) copy-start(f32[1,512,8]{2,1,0:T(8,128)S(1)} %copy.18) | copy-start | bytes 49156
  21.3 1.4 copy-start.15
  21.4 1.3 copy-start.17
  25.6 78.5 %collective-permute-start.3 = (f32[4,64,128]{2,1,0:T(8,128)}, f32[4,64,128]{2,1,0:T(8,128)}, u32[]{:S(2)}, u32[]{:S(2)}) collective-permute-start(f32[4,64,128]{2,1,0:T(8,128)} %bitcast.15), channel_id=1, source_target_pairs={{0,1},{1,2},{2,3},{3,4},{4,5},{5,6},{6,7},{7,8},{8,9},{9,10},{10,1... | collective-permute-start | bytes 393224 | tf_op jit(solution)/shard_map/ppermute | solution.py:17
  35.9 68.2 %collective-permute-start.2 = (f32[4,64,128]{2,1,0:T(8,128)}, f32[4,64,128]{2,1,0:T(8,128)}, u32[]{:S(2)}, u32[]{:S(2)}) collective-permute-start(f32[4,64,128]{2,1,0:T(8,128)} %bitcast.14), channel_id=1, source_target_pairs={{1,0},{2,1},{3,2},{4,3},{5,4},{6,5},{7,6},{8,7},{9,8},{10,9},{11,1... | collective-permute-start | bytes 393224 | tf_op jit(solution)/shard_map/ppermute | solution.py:19
  103.9 1.0 copy-start.7
  108.8 23.1 %copy-start.1 = (f32[65536]{0:T(1024)}, f32[65536]{0:T(1024)S(1)}, u32[]{:S(2)}) copy-start(f32[65536]{0:T(1024)S(1)} %fusion.156) | copy-start | bytes 786436
  108.8 23.3 %copy-start.13 = (s32[1,512,8]{2,1,0:T(8,128)S(1)}, s32[1,512,8]{2,1,0:T(8,128)}, u32[]{:S(2)}) copy-start(s32[1,512,8]{2,1,0:T(8,128)} %copy-done.12) | copy-start | bytes 49156
  108.8 242.7 %copy-start.27 = (f32[1,2,8]{2,1,0:T(2,128)S(1)}, f32[1,2,8]{2,1,0:T(2,128)}, u32[]{:S(2)}) copy-start(f32[1,2,8]{2,1,0:T(2,128)} %param.23) | copy-start | bytes 196
  108.8 265.0 %copy-start.20 = (f32[1,8,64,128]{3,2,1,0:T(8,128)S(1)}, f32[1,8,64,128]{3,2,1,0:T(8,128)}, u32[]{:S(2)}) copy-start(f32[1,8,64,128]{3,2,1,0:T(8,128)} %param.17) | copy-start | bytes 786436
  131.8 1.0 copy-start.9
  132.8 241.0 %copy-start.4 = (f32[2,8,64,128]{3,2,1,0:T(8,128)S(1)}, f32[2,8,64,128]{3,2,1,0:T(8,128)}, u32[]{:S(2)}) copy-start(f32[2,8,64,128]{3,2,1,0:T(8,128)} %copy-done.3) | copy-start | bytes 1572868
  132.8 241.0 %copy-start.11 = (f32[1,8,64,128]{3,2,1,0:T(8,128)S(1)}, f32[1,8,64,128]{3,2,1,0:T(8,128)}, u32[]{:S(2)}) copy-start(f32[1,8,64,128]{3,2,1,0:T(8,128)} %param.18) | copy-start | bytes 786436
  132.8 241.0 %copy-start.16 = (f32[2,4,64,128]{3,2,1,0:T(8,128)S(1)}, f32[2,4,64,128]{3,2,1,0:T(8,128)}, u32[]{:S(2)}) copy-start(f32[2,4,64,128]{3,2,1,0:T(8,128)} %copy-done.15) | copy-start | bytes 786436
  132.8 241.0 %copy-start.18 = (f32[2,4,64,128]{3,2,1,0:T(8,128)S(1)}, f32[2,4,64,128]{3,2,1,0:T(8,128)}, u32[]{:S(2)}) copy-start(f32[2,4,64,128]{3,2,1,0:T(8,128)} %copy-done.17) | copy-start | bytes 786436
  352.2 35.0 %all-to-all-start = ((f32[64,2,8]{2,1,0:T(2,128)}), f32[64,2,8]{2,1,0:T(2,128)S(1)}, u32[]{:S(2)}, u32[]{:S(2)}) async-start(f32[64,2,8]{2,1,0:T(2,128)} %stack.16), calls=%async_computation | async-start | bytes 131072 | tf_op jit(solution)/shard_map/all_to_all | solution.py:107
  373.8 127.9 %reduce-scatter.3.cloned.1.call-start = ((), (), s32[]{:S(2)}) async-start(), calls=%async_computation.2 | async-start | bytes 294912 | tf_op jit(solution)/shard_map/reduce_scatter | solution.py:118
  373.8 14.9 %copy-start.21 = (s32[4096,1]{0,1:T(1,128)S(1)}, s32[4096,1]{0,1:T(1,128)}, u32[]{:S(2)}) copy-start(s32[4096,1]{0,1:T(1,128)} %compare_select_fusion.1) | copy-start | bytes 49156
  388.0 0.7 copy-start.22
  417.2 6.9 %collective-permute-start.5 = (f32[4,64,128]{2,1,0:T(8,128)S(1)}, f32[4,64,128]{2,1,0:T(8,128)S(1)}, u32[]{:S(2)}, u32[]{:S(2)}) collective-permute-start(f32[4,64,128]{2,1,0:T(8,128)S(1)} %bitcast.182), channel_id=1, source_target_pairs={{0,1},{1,2},{2,3},{3,4},{4,5},{5,6},{6,7},{7,8},{8,9},{9,10},{10,1... | collective-permute-start | bytes 393224 | tf_op jit(solution)/shard_map/ppermute | solution.py:17
  419.6 6.9 %collective-permute-start.4 = (f32[4,64,128]{2,1,0:T(8,128)S(1)}, f32[4,64,128]{2,1,0:T(8,128)S(1)}, u32[]{:S(2)}, u32[]{:S(2)}) collective-permute-start(f32[4,64,128]{2,1,0:T(8,128)S(1)} %bitcast.181), channel_id=1, source_target_pairs={{1,0},{2,1},{3,2},{4,3},{5,4},{6,5},{7,6},{8,7},{9,8},{10,9},{11,1... | collective-permute-start | bytes 393224 | tf_op jit(solution)/shard_map/ppermute | solution.py:19
  427.1 28.4 %copy-start.14 = (f32[8,64,128]{2,1,0:T(8,128)S(1)}, f32[8,64,128]{2,1,0:T(8,128)}, u32[]{:S(2)}) copy-start(f32[8,64,128]{2,1,0:T(8,128)} %get-tuple-element.49) | copy-start | bytes 786436
  455.5 0.8 copy-start.2
  (4 other events, 2.7 us)
Sparse Core Ops, SparseCore 0:
  456.4 45.2 reduce-scatter.2
